TPU v7x, 32 devices: a whole 2x2x4 slice. The times are simulated.
32 devices in a mesh: run: 2 (over y), spec: 16 (over z, x, core).
Axes of the slice: x: 2, y: 2, z: 4, core: 2. Of those that a mesh axis runs over, the one named last changes fastest.
Arguments:
- tensor: bfloat16 [8, 2048, 8192], P('run', None, 'spec'), may hold values from -6 to 6
- run_factor: float32 [8, 64], P('run'), may hold values from -0.0625 to 0.0625
- mz_factor: float32 [8192, 64], P('spec'), may hold values from -6 to 6
Outputs:
- rt_factor: float32 [2048, 64], P('spec')
- mz_out: float32 [8192, 64], P('spec')
All inputs are finite; a program needn't handle non-finite values.
Results may differ from a plain program's by a relative error of at most 0.0052.
Values may be sent and summed in bfloat16 or wider, within the bound.
A program may use at most 64 MiB of HBM per device.

v0:
```python
import jax
import jax.numpy as jnp
from jax import lax
from jax.sharding import PartitionSpec as P

SWEEPS = 3


def solve_rows(gram, moment):
    lower = jnp.linalg.cholesky(gram)
    return jax.scipy.linalg.cho_solve((lower, True), moment.T).T


def shards(tensor, run_factor, mz_factor):
    highest = lax.Precision.HIGHEST
    run_gram = lax.psum(jnp.dot(run_factor.T, run_factor, precision=highest), "run")
    own_rows = tensor.shape[1] // lax.axis_size("spec")
    mz_now = mz_factor
    rt_factor = jnp.zeros((own_rows, run_factor.shape[1]), jnp.float32)
    for sweep_index in range(SWEEPS):
        mz_gram = lax.psum(jnp.dot(mz_now.T, mz_now, precision=highest), "spec")
        mz_half = mz_now.astype(jnp.bfloat16)
        proj = jnp.einsum("ijk,kr->ijr", tensor, mz_half, preferred_element_type=jnp.float32)
        share = lax.psum_scatter(
            jnp.einsum("ir,ijr->jr", run_factor, proj, precision=highest),
            "spec",
            scatter_dimension=0,
            tiled=True,
        )
        rt_moment = lax.psum(share, "run")
        rt_factor = solve_rows(run_gram * mz_gram, rt_moment)
        back = jnp.einsum(
            "ijk,jr->ikr",
            tensor,
            lax.all_gather(rt_factor.astype(jnp.bfloat16), "spec", axis=0, tiled=True),
            preferred_element_type=jnp.float32,
        )
        rt_gram = lax.psum(jnp.dot(rt_factor.T, rt_factor, precision=highest), "spec")
        partial_mz = jnp.einsum("ir,ikr->kr", run_factor, back, precision=highest)
        mz_moment = lax.psum(partial_mz, "run")
        mz_now = solve_rows(run_gram * rt_gram, mz_moment)
    return (rt_factor, mz_now)


def solution(mesh):
    return jax.shard_map(
        shards,
        mesh=mesh,
        in_specs=(P("run", None, "spec"), P("run", None), P("spec", None)),
        out_specs=(P("spec", None), P("spec", None)),
        check_vma=False,
    )
```

profile of v0, /device:TPU:0, one launch (start us, length us, event | category | flops | bytes accessed | tf_op | source)
XLA Modules:
  0.0 631.8 jit_solution(7266411907513488131)
XLA Ops:
  8.0 6.0 fusion.27
  19.7 63.0 %psum.92 = f32[64,64]{0,1:T(8,128)S(1)} all-reduce(f32[64,64]{0,1:T(8,128)S(1)} %fusion.76), channel_id=1, replica_groups=mesh['run'=2,'spec'=16] {'spec'}, use_global_device_ids=true, to_apply=%region_1.0 | all-reduce | flops 4096 | bytes 32768 | tf_op jit(solution)/shard_map/psum | solution.py:21
  83.0 9.5 %all-reduce = (f32[64,128]{1,0:T(8,128)S(1)}, f32[64,64]{0,1:T(8,128)S(1)}) all-reduce(f32[64,128]{1,0:T(8,128)} %bitcast.182, f32[64,64]{0,1:T(8,128)S(1)} %fusion.75), channel_id=1, replica_groups=mesh['run'=2,'spec'=16] {'run'}, use_global_device_ids=true, to_apply=%region_5.7 | all-reduce | flops 12288 | bytes 98304 | tf_op jit(solution)/shard_map/psum | solution.py:30
  92.6 5.8 cholesky.104
  105.3 57.6 %psum.94 = f32[64,64]{0,1:T(8,128)S(1)} all-reduce(f32[64,64]{0,1:T(8,128)S(1)} %fusion.77), channel_id=1, replica_groups=mesh['run'=2,'spec'=16] {'spec'}, use_global_device_ids=true, to_apply=%region_6.9 | all-reduce | flops 4096 | bytes 32768 | tf_op jit(solution)/shard_map/psum | solution.py:38
  163.0 5.8 cholesky.115
  169.5 17.8 %all_gather.9 = bf16[2048,64]{0,1:T(8,128)(2,1)S(1)} all-gather(bf16[128,64]{0,1:T(8,128)(2,1)S(1)} %convert_bitcast_fusion.1), channel_id=1, replica_groups=mesh['run'=2,'spec'=16] {'spec'}, dimensions={0}, use_global_device_ids=true | all-gather | bytes 278528 | tf_op jit(solution)/shard_map/all_gather | solution.py:35
  200.1 13.8 %all-reduce.5.cloned.1.call-done = f32[64,512]{1,0:T(8,128)} async-done(((f32[64,512]{1,0:T(8,128)}), f32[64,512]{1,0:T(8,128)}) %all-reduce.5.cloned.1.call-update) | async-done | bytes 131088 | tf_op jit(solution)/shard_map/psum | solution.py:40
  215.3 6.0 fusion.25
  227.0 60.8 %psum.96 = f32[64,64]{0,1:T(8,128)S(1)} all-reduce(f32[64,64]{0,1:T(8,128)S(1)} %fusion.78), channel_id=1, replica_groups=mesh['run'=2,'spec'=16] {'spec'}, use_global_device_ids=true, to_apply=%region_8.0 | all-reduce | flops 4096 | bytes 32768 | tf_op jit(solution)/shard_map/psum | solution.py:21
  287.9 5.8 cholesky.126
  300.0 8.1 %psum.97 = f32[64,128]{1,0:T(8,128)S(1)} all-reduce(f32[64,128]{1,0:T(8,128)} %bitcast.180), channel_id=1, replica_groups=mesh['run'=2,'spec'=16] {'run'}, use_global_device_ids=true, to_apply=%region_10.0 | all-reduce | flops 8192 | bytes 65536 | tf_op jit(solution)/shard_map/psum | solution.py:30
  308.8 57.6 %psum.98 = f32[64,64]{0,1:T(8,128)S(1)} all-reduce(f32[64,64]{0,1:T(8,128)S(1)} %fusion.79), channel_id=1, replica_groups=mesh['run'=2,'spec'=16] {'spec'}, use_global_device_ids=true, to_apply=%region_11.0 | all-reduce | flops 4096 | bytes 32768 | tf_op jit(solution)/shard_map/psum | solution.py:38
  366.5 5.8 cholesky.137
  373.0 17.8 %all_gather.10 = bf16[2048,64]{0,1:T(8,128)(2,1)S(1)} all-gather(bf16[128,64]{0,1:T(8,128)(2,1)S(1)} %convert_bitcast_fusion), channel_id=1, replica_groups=mesh['run'=2,'spec'=16] {'spec'}, dimensions={0}, use_global_device_ids=true | all-gather | bytes 278528 | tf_op jit(solution)/shard_map/all_gather | solution.py:35
  403.6 14.6 %all-reduce.7.cloned.1.call-done = f32[64,512]{1,0:T(8,128)} async-done(((f32[64,512]{1,0:T(8,128)}), f32[64,512]{1,0:T(8,128)}) %all-reduce.7.cloned.1.call-update) | async-done | bytes 131088 | tf_op jit(solution)/shard_map/psum | solution.py:40
  419.7 6.0 fusion.23
  431.4 60.7 %psum.100 = f32[64,64]{0,1:T(8,128)S(1)} all-reduce(f32[64,64]{0,1:T(8,128)S(1)} %fusion.80), channel_id=1, replica_groups=mesh['run'=2,'spec'=16] {'spec'}, use_global_device_ids=true, to_apply=%region_13.0 | all-reduce | flops 4096 | bytes 32768 | tf_op jit(solution)/shard_map/psum | solution.py:21
  492.3 5.8 cholesky.148
  504.4 8.1 %psum.101 = f32[64,128]{1,0:T(8,128)S(1)} all-reduce(f32[64,128]{1,0:T(8,128)} %bitcast.181), channel_id=1, replica_groups=mesh['run'=2,'spec'=16] {'run'}, use_global_device_ids=true, to_apply=%region_15.0 | all-reduce | flops 8192 | bytes 65536 | tf_op jit(solution)/shard_map/psum | solution.py:30
  513.1 57.6 %psum.102 = f32[64,64]{0,1:T(8,128)S(1)} all-reduce(f32[64,64]{0,1:T(8,128)S(1)} %fusion.81), channel_id=1, replica_groups=mesh['run'=2,'spec'=16] {'spec'}, use_global_device_ids=true, to_apply=%region_16.20 | all-reduce | flops 4096 | bytes 32768 | tf_op jit(solution)/shard_map/psum | solution.py:38
  570.8 5.8 cholesky.159
  577.3 18.1 %all_gather.11 = bf16[2048,64]{0,1:T(8,128)(2,1)S(1)} all-gather(bf16[128,64]{0,1:T(8,128)(2,1)S(1)} %bitcast_convert_fusion), channel_id=1, replica_groups=mesh['run'=2,'spec'=16] {'spec'}, dimensions={0}, use_global_device_ids=true | all-gather | bytes 278528 | tf_op jit(solution)/shard_map/all_gather | solution.py:35
  607.8 14.9 %all-reduce.9.cloned.1.call-done = f32[64,512]{1,0:T(8,128)} async-done(((f32[64,512]{1,0:T(8,128)}), f32[64,512]{1,0:T(8,128)}) %all-reduce.9.cloned.1.call-update) | async-done | bytes 131088 | tf_op jit(solution)/shard_map/psum | solution.py:40
  (101 shorter events, 84.1 us)
Async XLA Ops:
  7.2 75.8 %reduce-scatter.4.cloned.1.call-start = ((), (), s32[]{:S(2)}) async-start(), calls=%async_computation.3 | async-start | bytes 557056 | tf_op jit(solution)/shard_map/reduce_scatter | solution.py:24
  8.0 11.5 %copy-start = (f32[512,64]{0,1:T(8,128)S(1)}, f32[512,64]{0,1:T(8,128)}, u32[]{:S(2)}) copy-start(f32[512,64]{0,1:T(8,128)} %param.10) | copy-start | bytes 393220
  8.0 74.7 %copy-start.2 = (f32[4,64]{1,0:T(4,128)S(1)}, f32[4,64]{1,0:T(4,128)}, u32[]{:S(2)}) copy-start(f32[4,64]{1,0:T(4,128)} %param.9) | copy-start | bytes 3076
  19.4 194.4 %all-reduce.5.cloned.1.call-start = ((), (), s32[]{:S(2)}) async-start(), calls=%async_computation.4 | async-start | bytes 262144 | tf_op jit(solution)/shard_map/psum | solution.py:40
  194.3 105.7 %reduce-scatter.6.cloned.1.call-start = ((), (), s32[]{:S(2)}) async-start(), calls=%async_computation.5 | async-start | bytes 557056 | tf_op jit(solution)/shard_map/reduce_scatter | solution.py:24
  226.7 191.5 %all-reduce.7.cloned.1.call-start = ((), (), s32[]{:S(2)}) async-start(), calls=%async_computation.6 | async-start | bytes 262144 | tf_op jit(solution)/shard_map/psum | solution.py:40
  397.8 106.6 %reduce-scatter.8.cloned.1.call-start = ((), (), s32[]{:S(2)}) async-start(), calls=%async_computation.7 | async-start | bytes 557056 | tf_op jit(solution)/shard_map/reduce_scatter | solution.py:24
  431.1 191.7 %all-reduce.9.cloned.1.call-start = ((), (), s32[]{:S(2)}) async-start(), calls=%async_computation.8 | async-start | bytes 262144 | tf_op jit(solution)/shard_map/psum | solution.py:40
  512.9 112.1 %copy-start.1 = (f32[64,128]{1,0:T(8,128)}, f32[64,128]{1,0:T(8,128)S(1)}, u32[]{:S(2)}) copy-start(f32[64,128]{1,0:T(8,128)S(1)} %fusion.42) | copy-start | bytes 98308
Sparse Core Ops, SparseCore 0:
  19.5 58.4 reduce-scatter.3
  194.4 19.3 all-reduce.4
  226.8 55.8 reduce-scatter.5
  397.9 20.2 all-reduce.6
  431.2 55.7 reduce-scatter.7
  602.5 20.2 all-reduce.8
where the time goes:
time: 633 us; the launch traced here: 632 us
  blocking collectives  437 us (69%)
  other arithmetic  72.4 us (11%)
  matrix products  57.8 us (9%)
  waiting for transfers between devices  43.5 us (7%)
  between operations  14.5 us (2%)
    psum x3, blocking collectives, shards(): mz_gram = lax.psum(jnp.dot(mz_now.T, mz_now, precision=highest), 'spec')  184 us
    psum x3, blocking collectives, shards(): lax.psum(jnp.dot(rt_factor.T, rt_factor, precision=highest), 'spec')  173 us
    all_gather x3, blocking collectives, shards(): lax.all_gather(rt_factor.astype(jnp.bfloat16), 'spec', axis=0, tiled=True)  53.7 us
    psum x3, waiting for transfers between devices, shards(): mz_moment = lax.psum(partial_mz, 'run')  43.3 us
    another operation x18, other arithmetic, solve_rows(): lower = jnp.linalg.cholesky(gram)  39.1 us
    another operation x12, other arithmetic, solve_rows(): return jax.scipy.linalg.cho_solve((lower, True), moment.T).T  33.2 us
    psum x3, blocking collectives, shards(): rt_moment = lax.psum(share, 'run')  25.6 us
    dot_general x3, matrix products, shards(): jnp.einsum('ijk,kr->ijr', tensor, mz_half, preferred_element_type=jnp.flo...  18 us
  transfers between devices with their start and end apart: 6, of which 3 were waited for; matrix products, arithmetic and copies ran while one was open for 7% of the time, Pallas kernels for 0%

commit v1 on v0

v1 whole, which is shorter than its diff:
```python
import functools

import jax
import jax.numpy as jnp
from jax import lax
from jax.experimental import pallas as pl
from jax.experimental.pallas import tpu as pltpu
from jax.sharding import PartitionSpec as P

SWEEPS = 3
ZDIM = 4
PARTS = 2
HIGHEST = lax.Precision.HIGHEST
F32 = jnp.float32
BF16 = jnp.bfloat16
NT = (((1,), (1,)), ((), ()))
TN = (((0,), (0,)), ((), ()))


def negative_inverse(a):
    n = a.shape[0]
    lanes = lax.broadcasted_iota(jnp.int32, (1, n), 1)
    rows = lax.broadcasted_iota(jnp.int32, (n, 1), 0)
    for p in range(n):
        col = a[:, p : p + 1]
        row = a[p : p + 1, :]
        inv = 1.0 / a[p : p + 1, p : p + 1]
        here = lanes == p
        scaled = jnp.where(here, 0.0, row * inv)
        keep = jnp.where(here, 0.0, a)
        swept = keep - col * scaled + jnp.where(here, col * inv, 0.0)
        pivot_row = scaled + jnp.where(here, -inv, 0.0)
        a = jnp.where(rows == p, pivot_row, swept)
    return a


def kernel(
    runs, xdim, t_hbm, rf_ref, rft_ref, mz_in, rt_out, mz_out,
    t_ref, mz_ref, half_ref, w_ref, rf_all, gram_own, gram_a, gram_sum, gram_b,
    mom, mom_c, red_c, mom_x, red_x, mom_z, mom_r, rt_all, mzs,
    load_sem, rf_sem, ga_sem, gb_sem, c_sem, x_sem, z_sem, r_sem, az_sem, ax_sem, ac_sem, m_sem,
):
    r = lax.axis_index("run")
    s = lax.axis_index("spec")
    c = lax.rem(s, 2)
    x = lax.rem(s // 2, xdim)
    z = s // (2 * xdim)
    local_runs, width = t_ref.shape[0], rt_out.shape[1]
    rank, mz_rows = mz_in.shape
    part = mz_rows // PARTS

    load = pltpu.make_async_copy(t_hbm, t_ref, load_sem)
    load.start()

    core_peer = s + 1 - 2 * c
    x_peers = [(lax.rem(x + d, xdim) - x) * 2 + s for d in range(1, xdim)]
    z_peers = [(lax.rem(z + d, ZDIM) - z) * 2 * xdim + s for d in range(1, ZDIM)]
    run_peers = [lax.rem(r + d, runs) for d in range(1, runs)]
    inner = lax.rem(s, 2 * xdim)
    inner_peers = [s - inner + lax.rem(inner + d, 2 * xdim) for d in range(1, 2 * xdim)]

    everyone = [(r, q) for q in inner_peers + z_peers] + [(q, s) for q in run_peers]
    barrier = pltpu.get_barrier_semaphore()
    for peer in everyone:
        pl.semaphore_signal(barrier, inc=1, device_id=peer, device_id_type=pl.DeviceIdType.MESH)
    pl.semaphore_wait(barrier, len(everyone))

    def send(src, dst, sems, index, peer):
        copy = pltpu.make_async_remote_copy(
            src_ref=src, dst_ref=dst, send_sem=sems.at[(0,) + index], recv_sem=sems.at[(1,) + index],
            device_id=peer, device_id_type=pl.DeviceIdType.MESH,
        )
        copy.start()
        return copy

    rf_all[r] = rf_ref[...]
    rf_copies = [send(rf_all.at[r], rf_all.at[r], rf_sem, (d,), (q, s)) for d, q in enumerate(run_peers)]
    mz_ref[...] = mz_in[...]
    for i in range(local_runs):
        w_ref[i] = jnp.broadcast_to(rft_ref[:, i : i + 1], w_ref.shape[1:])
    for copy in rf_copies:
        copy.wait()
    run_gram = jnp.zeros((rank, rank), F32)
    for i in range(runs):
        run_gram += lax.dot_general(rf_all[i], rf_all[i], TN, precision=HIGHEST, preferred_element_type=F32)
    load.wait()

    def sweep(n, run_gram):
        mz_now = mz_ref[...]
        gram_own[n] = lax.dot_general(mz_now, mz_now, NT, precision=HIGHEST, preferred_element_type=F32)
        ga = [send(gram_own.at[n], gram_a.at[n, d], ga_sem, (n, d), (r, q)) for d, q in enumerate(inner_peers)]
        half_ref[...] = mz_now.astype(BF16)

        def project(cc):
            for xx in range(xdim):
                for zz in range(0, ZDIM, 2):
                    total = jnp.zeros((rank, 2 * width), F32)
                    starts = [
                        pl.multiple_of((((zz + e) * xdim + xx) * 2 + cc) * width, width) for e in range(2)
                    ]
                    for i in range(local_runs):
                        slab = jnp.concatenate([t_ref[i, pl.ds(at, width), :] for at in starts], axis=0)
                        proj = lax.dot_general(half_ref[...], slab, NT, preferred_element_type=F32)
                        total += proj * jnp.concatenate([w_ref[i][:, :width]] * 2, axis=1)
                    mom[n, cc, xx, zz] = total[:, :width]
                    mom[n, cc, xx, zz + 1] = total[:, width:]

        project(1 - c)
        to_core = send(mom.at[n, 1 - c], mom_c.at[n], c_sem, (n,), (r, core_peer))
        project(c)
        for copy in ga:
            copy.wait()
        total = gram_own[n]
        for d in range(len(ga)):
            total += gram_a[n, d]
        gram_sum[n] = total
        gb = [send(gram_sum.at[n], gram_b.at[n, d], gb_sem, (n, d), (r, q)) for d, q in enumerate(z_peers)]
        to_core.wait()
        red_c[n] = mom[n, c] + mom_c[n]
        to_x = []
        for d, q in enumerate(x_peers):
            to_x.append(send(red_c.at[n, lax.rem(x + d + 1, xdim)], mom_x.at[n, d], x_sem, (n, d), (r, q)))
        for copy in gb:
            copy.wait()
        total = gram_sum[n]
        for d in range(len(gb)):
            total += gram_b[n, d]
        inverse = negative_inverse(run_gram * total)
        for copy in to_x:
            copy.wait()
        total = red_c[n, x]
        for d in range(len(to_x)):
            total += mom_x[n, d]
        red_x[n] = total
        to_z = []
        for d, q in enumerate(z_peers):
            to_z.append(send(red_x.at[n, lax.rem(z + d + 1, ZDIM)], mom_z.at[n, d], z_sem, (n, d), (r, q)))
        for copy in to_z:
            copy.wait()
        total = red_x[n, z]
        for d in range(len(to_z)):
            total += mom_z[n, d]
        mom_r[n, r] = total
        to_r = [send(mom_r.at[n, r], mom_r.at[n, r], r_sem, (n, d), (q, s)) for d, q in enumerate(run_peers)]
        for copy in to_r:
            copy.wait()
        total = mom_r[n, 0]
        for d in range(1, runs):
            total += mom_r[n, d]
        rt = -jnp.dot(inverse, total, precision=HIGHEST, preferred_element_type=F32)
        rt_out[...] = rt

        rt_all[n, c, x, z] = rt.astype(BF16)
        own = rt_all.at[n, c, x, z]
        copies = [send(own, own, az_sem, (n, d), (r, q)) for d, q in enumerate(z_peers)]
        for copy in copies:
            copy.wait()
        own = rt_all.at[n, c, x]
        copies = [send(own, own, ax_sem, (n, d), (r, q)) for d, q in enumerate(x_peers)]
        for copy in copies:
            copy.wait()
        own = rt_all.at[n, c]
        send(own, own, ac_sem, (n,), (r, core_peer)).wait()
        rt_half = jnp.concatenate(
            [rt_all[n, p % 2, p // 2 % xdim, p // (2 * xdim)] for p in range(2 * xdim * ZDIM)], axis=1
        )
        rt_gram = lax.dot_general(rt_half, rt_half, NT, preferred_element_type=F32)
        copies = []
        for h in range(PARTS):
            total = jnp.zeros((rank, part), F32)
            for i in range(local_runs):
                back = jnp.dot(rt_half, t_ref[i, :, h * part : (h + 1) * part], preferred_element_type=F32)
                total += back * jnp.concatenate([w_ref[i]] * (part // 128), axis=1)
            mzs[n, r, h] = total
            for d, q in enumerate(run_peers):
                copies.append(send(mzs.at[n, r, h], mzs.at[n, r, h], m_sem, (n, h, d), (q, s)))
        inverse = negative_inverse(run_gram * rt_gram)
        for copy in copies:
            copy.wait()
        for h in range(PARTS):
            total = mzs[n, 0, h]
            for d in range(1, runs):
                total += mzs[n, d, h]
            mz_ref[:, h * part : (h + 1) * part] = -jnp.dot(
                inverse, total, precision=HIGHEST, preferred_element_type=F32
            )
        return run_gram

    lax.fori_loop(0, SWEEPS, sweep, run_gram)
    mz_out[...] = mz_ref[...]


def shards(tensor, run_factor, mz_factor):
    runs, spec = lax.axis_size("run"), lax.axis_size("spec")
    xdim = spec // (2 * ZDIM)
    local_runs, rt_rows, mz_rows = tensor.shape
    rank = run_factor.shape[1]
    width = rt_rows // spec
    part = mz_rows // PARTS
    vmem = pl.BlockSpec(memory_space=pltpu.VMEM)
    square = (rank, rank)
    dma = pltpu.SemaphoreType.DMA
    near, far, line = max(xdim - 1, 1), ZDIM - 1, max(runs - 1, 1)
    rt_factor, mz_out = pl.pallas_call(
        functools.partial(kernel, runs, xdim),
        out_shape=(
            jax.ShapeDtypeStruct((rank, width), F32),
            jax.ShapeDtypeStruct((rank, mz_rows), F32),
        ),
        in_specs=[pl.BlockSpec(memory_space=pl.ANY), vmem, vmem, vmem],
        out_specs=(vmem, vmem),
        scratch_shapes=[
            pltpu.VMEM(tensor.shape, BF16),
            pltpu.VMEM((rank, mz_rows), F32),
            pltpu.VMEM((rank, mz_rows), BF16),
            pltpu.VMEM((local_runs, rank, 128), F32),
            pltpu.VMEM((runs, local_runs, rank), F32),
            pltpu.VMEM((SWEEPS,) + square, F32),
            pltpu.VMEM((SWEEPS, 2 * xdim - 1) + square, F32),
            pltpu.VMEM((SWEEPS,) + square, F32),
            pltpu.VMEM((SWEEPS, far) + square, F32),
            pltpu.VMEM((SWEEPS, 2, xdim, ZDIM, rank, width), F32),
            pltpu.VMEM((SWEEPS, xdim, ZDIM, rank, width), F32),
            pltpu.VMEM((SWEEPS, xdim, ZDIM, rank, width), F32),
            pltpu.VMEM((SWEEPS, near, ZDIM, rank, width), F32),
            pltpu.VMEM((SWEEPS, ZDIM, rank, width), F32),
            pltpu.VMEM((SWEEPS, far, rank, width), F32),
            pltpu.VMEM((SWEEPS, runs, rank, width), F32),
            pltpu.VMEM((SWEEPS, 2, xdim, ZDIM, rank, width), BF16),
            pltpu.VMEM((SWEEPS, runs, PARTS, rank, part), F32),
            dma,
            dma((2, line)),
            dma((2, SWEEPS, 2 * xdim - 1)),
            dma((2, SWEEPS, far)),
            dma((2, SWEEPS)),
            dma((2, SWEEPS, near)),
            dma((2, SWEEPS, far)),
            dma((2, SWEEPS, line)),
            dma((2, SWEEPS, far)),
            dma((2, SWEEPS, near)),
            dma((2, SWEEPS)),
            dma((2, SWEEPS, PARTS, line)),
        ],
        compiler_params=pltpu.CompilerParams(
            collective_id=0, has_side_effects=True, vmem_limit_bytes=56 * 1024 * 1024
        ),
    )(tensor, run_factor, run_factor.T, mz_factor.T)
    return rt_factor.T, mz_out.T


def solution(mesh):
    return jax.shard_map(
        shards,
        mesh=mesh,
        in_specs=(P("run", None, "spec"), P("run", None), P("spec", None)),
        out_specs=(P("spec", None), P("spec", None)),
        check_vma=False,
    )
```

time: 633 us -> 135 us (0.21)
  blocking collectives: 437 us -> 0 us
  Pallas kernels: 0 us -> 129 us
  other arithmetic: 72.4 us -> 0 us
  matrix products: 57.8 us -> 0 us
  waiting for transfers between devices: 43.5 us -> 0 us
  between operations: 14.5 us -> 0.64 us
    psum x9 -> x0, blocking collectives: 383 us -> none  [the longest x3 184 us: shards(): mz_gram = lax.psum(jnp.dot(mz_now.T, mz_now, precision=highest), 'spec')]
    pallas_call x0 -> x1, Pallas kernels: none -> 129 us  [shards(): pl.pallas_call(functools.partial(kernel, runs, xdim), out_shape=(jax.Shap...]
    another operation x30 -> x0, other arithmetic: 72.3 us -> none  [the longest x18 39.1 us: solve_rows(): lower = jnp.linalg.cholesky(gram)]
    all_gather x3 -> x0, blocking collectives: 53.7 us -> none  [shards(): lax.all_gather(rt_factor.astype(jnp.bfloat16), 'spec', axis=0, tiled=True)]
    dot_general x19 -> x0, matrix products: 51.5 us -> none  [the longest x3 18 us: shards(): jnp.einsum('ijk,kr->ijr', tensor, mz_half, preferred_element_type=jnp.flo...]
    psum x3 -> x0, waiting for transfers between devices: 43.3 us -> none  [shards(): mz_moment = lax.psum(partial_mz, 'run')]
  transfers between devices with their start and end apart: 6 -> 0, of which waited for: 3 -> 0; matrix products, arithmetic and copies ran while one was open for 7% -> 0% of each run, Pallas kernels for 0% -> 0%
where the time goes in v1:
time: 135 us; the launch traced here: 134 us
  Pallas kernels  129 us (96%)
  local copies, waits for them, and re-layouts  4.33 us (3%)
    pallas_call x1, Pallas kernels, shards(): pl.pallas_call(functools.partial(kernel, runs, xdim), out_shape=(jax.Shap...  129 us
    unnamed x3, local copies, waits for them, and re-layouts  4.33 us

profile of v1, /device:TPU:0, one launch (start us, length us, event | category | flops | bytes accessed | tf_op | source)
XLA Modules:
  0.0 134.4 jit_solution(8705316345646437486)
XLA Ops:
  0.6 1.4 %copy.5 = f32[4,64]{0,1:T(8,128)} copy(f32[4,64]{1,0:T(4,128)} %rf_ref.1) | data formatting | bytes 2048 | tf_op args[1]
  2.0 129.4 %shard_map.50 = (f32[64,128]{1,0:T(8,128)}, f32[64,512]{1,0:T(8,128)}) custom-call(bf16[4,2048,512]{2,1,0:T(8,128)(2,1)} %t_hbm.1, f32[4,64]{1,0:T(4,128)} %rf_ref.1, f32[64,4]{1,0:T(8,128)} %bitcast.5, f32[64,512]{1,0:T(8,128)} %bitcast.4), custom_call_target="tpu_custom_call" | custom-call | tf_op jit(solution)/shard_map/pallas_call | solution.py:204
  131.4 1.4 %copy.8 = f32[128,64]{0,1:T(8,128)} copy(f32[128,64]{0,1:T(8,128)} %bitcast.7) | data formatting | bytes 65536
  132.8 1.6 %copy.9 = f32[512,64]{0,1:T(8,128)} copy(f32[512,64]{0,1:T(8,128)} %bitcast.6) | data formatting | bytes 262144

commit v2 on v1

v2 whole, which is shorter than its diff:
```python
import functools

import jax
import jax.numpy as jnp
from jax import lax
from jax.experimental import pallas as pl
from jax.experimental.pallas import tpu as pltpu
from jax.sharding import PartitionSpec as P

SWEEPS = 3
ZDIM = 4
PARTS = 2
HIGHEST = lax.Precision.HIGHEST
F32 = jnp.float32
BF16 = jnp.bfloat16
NT = (((1,), (1,)), ((), ()))
TN = (((0,), (0,)), ((), ()))


def sweep_pairs(a, blocks):
    n = a.shape[0]
    lanes = lax.broadcasted_iota(jnp.int32, (1, n), 1)
    rows = lax.broadcasted_iota(jnp.int32, (n, 1), 0)

    def block(_, a):
        for p in range(0, 8, 2):
            q = p + 1
            c1 = jnp.broadcast_to(a[:, p : p + 1], (n, n))
            c2 = jnp.broadcast_to(a[:, q : q + 1], (n, n))
            b = c1[q : q + 1, :]
            inv = 1.0 / c1[p : p + 1, :]
            ratio = b * inv
            s22 = 1.0 / (c2[q : q + 1, :] - b * ratio)
            s12 = -ratio * s22
            s11 = inv - ratio * s12
            r1, r2 = a[p : p + 1, :], a[q : q + 1, :]
            h1, h2 = lanes == p, lanes == q
            m1 = jnp.where(h1, -s11, jnp.where(h2, -s12, s11 * r1 + s12 * r2))
            m2 = jnp.where(h1, -s12, jnp.where(h2, -s22, s12 * r1 + s22 * r2))
            swept = jnp.where(h1 | h2, 0.0, a) - c1 * m1 - c2 * m2
            a = jnp.where(rows == p, m1, jnp.where(rows == q, m2, swept))
        a = jnp.concatenate([a[8:], a[:8]], axis=0)
        return jnp.concatenate([a[:, 8:], a[:, :8]], axis=1)

    return lax.fori_loop(0, blocks, block, a)


def pack(g):
    half = g.shape[0] // 2
    return jnp.concatenate([g[:half], g[half:]], axis=1)


def unpack(g):
    half = g.shape[1] // 2
    return jnp.concatenate([g[:, :half], g[:, half:]], axis=0)


def kernel(
    runs, xdim, t_hbm, rf_ref, rft_ref, mz_in, rt_out, mz_out,
    t_ref, mz_ref, half_ref, w_ref, rf_all, gram_own, gram_a, gram_sum, gram_b,
    mom, mom_c, red_c, mom_x, red_x, mom_zr, rt_all, mzs, inv_ref,
    load_sem, rf_sem, ga_sem, gb_sem, c_sem, x_sem, zr_sem, az_sem, ax_sem, m_sem,
):
    r = lax.axis_index("run")
    s = lax.axis_index("spec")
    c = lax.rem(s, 2)
    x = lax.rem(s // 2, xdim)
    z = s // (2 * xdim)
    local_runs, width = t_ref.shape[0], rt_out.shape[1]
    rank, mz_rows = mz_in.shape
    part = mz_rows // PARTS

    load = pltpu.make_async_copy(t_hbm, t_ref, load_sem)
    load.start()

    core_peer = s + 1 - 2 * c
    x_peers = [(lax.rem(x + d, xdim) - x) * 2 + s for d in range(1, xdim)]
    z_peers = [(lax.rem(z + d, ZDIM) - z) * 2 * xdim + s for d in range(1, ZDIM)]
    run_peers = [lax.rem(r + d, runs) for d in range(1, runs)]
    inner = lax.rem(s, 2 * xdim)
    inner_peers = [s - inner + lax.rem(inner + d, 2 * xdim) for d in range(1, 2 * xdim)]

    zr_peers = []
    for e in range(runs):
        for d in range(ZDIM):
            if e or d:
                zz = lax.rem(z + d, ZDIM)
                zr_peers.append((zz, (lax.rem(r + e, runs), s + (zz - z) * 2 * xdim)))

    everyone = [(r, q) for q in inner_peers] + [peer for _, peer in zr_peers]
    barrier = pltpu.get_barrier_semaphore()
    for peer in everyone:
        pl.semaphore_signal(barrier, inc=1, device_id=peer, device_id_type=pl.DeviceIdType.MESH)
    pl.semaphore_wait(barrier, len(everyone))

    def send(src, dst, sems, index, peer):
        copy = pltpu.make_async_remote_copy(
            src_ref=src, dst_ref=dst, send_sem=sems.at[(0,) + index], recv_sem=sems.at[(1,) + index],
            device_id=peer, device_id_type=pl.DeviceIdType.MESH,
        )
        copy.start()
        return copy

    rf_all[r] = rf_ref[...]
    rf_copies = [send(rf_all.at[r], rf_all.at[r], rf_sem, (d,), (q, s)) for d, q in enumerate(run_peers)]
    mz_ref[...] = mz_in[...]
    for i in range(local_runs):
        w_ref[i] = jnp.broadcast_to(rft_ref[:, i : i + 1], w_ref.shape[1:])
    for copy in rf_copies:
        copy.wait()
    run_gram = jnp.zeros((rank, rank), F32)
    for i in range(runs):
        run_gram += lax.dot_general(rf_all[i], rf_all[i], TN, precision=HIGHEST, preferred_element_type=F32)
    load.wait()

    def sweep(n, run_gram):
        mz_now = mz_ref[...]
        gram = lax.dot_general(mz_now, mz_now, NT, precision=HIGHEST, preferred_element_type=F32)
        gram_own[n] = pack(gram)
        ga = [send(gram_own.at[n], gram_a.at[n, d], ga_sem, (n, d), (r, q)) for d, q in enumerate(inner_peers)]
        half_ref[...] = mz_now.astype(BF16)

        def project(cc, xx):
            for zz in range(0, ZDIM, 2):
                total = jnp.zeros((rank, 2 * width), F32)
                starts = [pl.multiple_of((((zz + e) * xdim + xx) * 2 + cc) * width, width) for e in range(2)]
                for i in range(local_runs):
                    slab = jnp.concatenate([t_ref[i, pl.ds(at, width), :] for at in starts], axis=0)
                    proj = lax.dot_general(half_ref[...], slab, NT, preferred_element_type=F32)
                    total += proj * jnp.concatenate([w_ref[i][:, :width]] * 2, axis=1)
                mom[n, cc, xx, zz] = total[:, :width]
                mom[n, cc, xx, zz + 1] = total[:, width:]

        for xx in range(xdim):
            project(1 - c, xx)
        to_core = send(mom.at[n, 1 - c], mom_c.at[n], c_sem, (n,), (r, core_peer))
        others = [lax.rem(x + d, xdim) for d in range(1, xdim)]
        for xx in others:
            project(c, xx)
        for copy in ga:
            copy.wait()
        total = gram_own[n]
        for d in range(len(ga)):
            total += gram_a[n, d]
        gram_sum[n] = total
        gb = [send(gram_sum.at[n], gram_b.at[n, d], gb_sem, (n, d), (r, q)) for d, q in enumerate(z_peers)]
        to_core.wait()
        to_x = []
        for d, xx in enumerate(others):
            red_c[n, xx] = mom[n, c, xx] + mom_c[n, xx]
            to_x.append(send(red_c.at[n, xx], mom_x.at[n, d], x_sem, (n, d), (r, x_peers[d])))
        project(c, x)
        for copy in gb:
            copy.wait()
        total = gram_sum[n]
        for d in range(len(gb)):
            total += gram_b[n, d]
        inv_ref[...] = sweep_pairs(run_gram * unpack(total), rank // 16)
        for copy in to_x:
            copy.wait()
        total = mom[n, c, x] + mom_c[n, x]
        for d in range(len(to_x)):
            total += mom_x[n, d]
        red_x[n] = total
        to_zr = [
            send(red_x.at[n, zz], mom_zr.at[n, r, z], zr_sem, (n, d), peer)
            for d, (zz, peer) in enumerate(zr_peers)
        ]
        mom_zr[n, r, z] = red_x[n, z]
        inv_ref[...] = sweep_pairs(inv_ref[...], rank // 16)
        for copy in to_zr:
            copy.wait()
        total = jnp.zeros((rank, width), F32)
        for e in range(runs):
            for d in range(ZDIM):
                total += mom_zr[n, e, d]
        rt = -jnp.dot(inv_ref[...], total, precision=HIGHEST, preferred_element_type=F32)
        rt_out[...] = rt

        rt_all[n, c, x, z] = rt.astype(BF16)
        own = rt_all.at[n, c, x, z]
        copies = [send(own, own, az_sem, (n, d), (r, q)) for d, q in enumerate(z_peers)]
        for copy in copies:
            copy.wait()
        own = rt_all.at[n, c, x]
        copies = [send(own, own, ax_sem, (n, d), (r, q)) for d, q in enumerate(inner_peers)]
        for copy in copies:
            copy.wait()
        rt_half = jnp.concatenate(
            [rt_all[n, p % 2, p // 2 % xdim, p // (2 * xdim)] for p in range(2 * xdim * ZDIM)], axis=1
        )
        rt_gram = lax.dot_general(rt_half, rt_half, NT, preferred_element_type=F32)
        copies = []
        for h in range(PARTS):
            total = jnp.zeros((rank, part), F32)
            for i in range(local_runs):
                back = jnp.dot(rt_half, t_ref[i, :, h * part : (h + 1) * part], preferred_element_type=F32)
                total += back * jnp.concatenate([w_ref[i]] * (part // 128), axis=1)
            mzs[n, r, h] = total
            for d, q in enumerate(run_peers):
                copies.append(send(mzs.at[n, r, h], mzs.at[n, r, h], m_sem, (n, h, d), (q, s)))
        inv_ref[...] = sweep_pairs(run_gram * rt_gram, rank // 8)
        for copy in copies:
            copy.wait()
        for h in range(PARTS):
            total = mzs[n, 0, h]
            for d in range(1, runs):
                total += mzs[n, d, h]
            mz_ref[:, h * part : (h + 1) * part] = -jnp.dot(
                inv_ref[...], total, precision=HIGHEST, preferred_element_type=F32
            )
        return run_gram

    lax.fori_loop(0, SWEEPS, sweep, run_gram)
    mz_out[...] = mz_ref[...]


def shards(tensor, run_factor, mz_factor):
    runs, spec = lax.axis_size("run"), lax.axis_size("spec")
    xdim = spec // (2 * ZDIM)
    local_runs, rt_rows, mz_rows = tensor.shape
    rank = run_factor.shape[1]
    width = rt_rows // spec
    part = mz_rows // PARTS
    vmem = pl.BlockSpec(memory_space=pltpu.VMEM)
    square, packed = (rank, rank), (rank // 2, 2 * rank)
    dma = pltpu.SemaphoreType.DMA
    near, far, line = max(xdim - 1, 1), ZDIM - 1, max(runs - 1, 1)
    rt_factor, mz_out = pl.pallas_call(
        functools.partial(kernel, runs, xdim),
        out_shape=(
            jax.ShapeDtypeStruct((rank, width), F32),
            jax.ShapeDtypeStruct((rank, mz_rows), F32),
        ),
        in_specs=[pl.BlockSpec(memory_space=pl.ANY), vmem, vmem, vmem],
        out_specs=(vmem, vmem),
        scratch_shapes=[
            pltpu.VMEM(tensor.shape, BF16),
            pltpu.VMEM((rank, mz_rows), F32),
            pltpu.VMEM((rank, mz_rows), BF16),
            pltpu.VMEM((local_runs, rank, 128), F32),
            pltpu.VMEM((runs, local_runs, rank), F32),
            pltpu.VMEM((SWEEPS,) + packed, F32),
            pltpu.VMEM((SWEEPS, 2 * xdim - 1) + packed, F32),
            pltpu.VMEM((SWEEPS,) + packed, F32),
            pltpu.VMEM((SWEEPS, far) + packed, F32),
            pltpu.VMEM((SWEEPS, 2, xdim, ZDIM, rank, width), F32),
            pltpu.VMEM((SWEEPS, xdim, ZDIM, rank, width), F32),
            pltpu.VMEM((SWEEPS, xdim, ZDIM, rank, width), F32),
            pltpu.VMEM((SWEEPS, near, ZDIM, rank, width), F32),
            pltpu.VMEM((SWEEPS, ZDIM, rank, width), F32),
            pltpu.VMEM((SWEEPS, runs, ZDIM, rank, width), F32),
            pltpu.VMEM((SWEEPS, 2, xdim, ZDIM, rank, width), BF16),
            pltpu.VMEM((SWEEPS, runs, PARTS, rank, part), F32),
            pltpu.VMEM(square, F32),
            dma,
            dma((2, line)),
            dma((2, SWEEPS, 2 * xdim - 1)),
            dma((2, SWEEPS, far)),
            dma((2, SWEEPS)),
            dma((2, SWEEPS, near)),
            dma((2, SWEEPS, runs * ZDIM - 1)),
            dma((2, SWEEPS, far)),
            dma((2, SWEEPS, 2 * xdim - 1)),
            dma((2, SWEEPS, PARTS, line)),
        ],
        compiler_params=pltpu.CompilerParams(
            collective_id=0, has_side_effects=True, vmem_limit_bytes=56 * 1024 * 1024
        ),
    )(tensor, run_factor, run_factor.T, mz_factor.T)
    return rt_factor.T, mz_out.T


def solution(mesh):
    return jax.shard_map(
        shards,
        mesh=mesh,
        in_specs=(P("run", None, "spec"), P("run", None), P("spec", None)),
        out_specs=(P("spec", None), P("spec", None)),
        check_vma=False,
    )
```

time: 135 us -> 107 us (0.79)
  Pallas kernels: 129 us -> 102 us
    pallas_call x1, Pallas kernels: 129 us -> 102 us  [shards(): pl.pallas_call(functools.partial(kernel, runs, xdim), out_shape=(jax.Shap...]
where the time goes in v2:
time: 107 us
  Pallas kernels  102 us (95%)
  local copies, waits for them, and re-layouts  4.33 us (4%)
    pallas_call x1, Pallas kernels, shards(): pl.pallas_call(functools.partial(kernel, runs, xdim), out_shape=(jax.Shap...  102 us
    unnamed x3, local copies, waits for them, and re-layouts  4.33 us

profile of v2, /device:TPU:0, one launch (start us, length us, event | category | flops | bytes accessed | tf_op | source)
XLA Modules:
  0.0 106.9 jit_solution(14545676851113257531)
XLA Ops:
  0.6 1.4 %copy.5 = f32[4,64]{0,1:T(8,128)} copy(f32[4,64]{1,0:T(4,128)} %rf_ref.1) | data formatting | bytes 2048 | tf_op args[1]
  2.0 102.0 %shard_map.50 = (f32[64,128]{1,0:T(8,128)}, f32[64,512]{1,0:T(8,128)}) custom-call(bf16[4,2048,512]{2,1,0:T(8,128)(2,1)} %t_hbm.1, f32[4,64]{1,0:T(4,128)} %rf_ref.1, f32[64,4]{1,0:T(8,128)} %bitcast.5, f32[64,512]{1,0:T(8,128)} %bitcast.4), custom_call_target="tpu_custom_call" | custom-call | tf_op jit(solution)/shard_map/pallas_call | solution.py:229
  104.0 1.4 %copy.8 = f32[128,64]{0,1:T(8,128)} copy(f32[128,64]{0,1:T(8,128)} %bitcast.7) | data formatting | bytes 65536
  105.4 1.6 %copy.9 = f32[512,64]{0,1:T(8,128)} copy(f32[512,64]{0,1:T(8,128)} %bitcast.6) | data formatting | bytes 262144
